TPU v7x, 32 devices: a whole 2x2x4 slice. The times are simulated.
32 devices in a mesh: vin: 8 (over z, core), vout: 2 (over x), cell: 2 (over y).
Axes of the slice: x: 2, y: 2, z: 4, core: 2. Of those that a mesh axis runs over, the one named last changes fastest.
Arguments:
- distribution: bfloat16 [8, 13824, 4, 128], P('vout', 'vin', 'cell'), may hold values from -6 to 6
- collision: bfloat16 [13824, 13824], P('vout', 'vin'), may hold values from -1 to 3
- speeds: float32 [3, 13824], P(None, 'vout'), may hold values from 0.05 to 0.3
- directions: int32 [3, 13824], P(None, 'vout'), may hold values from 0 to 1
- cell_flags: int32 [8, 4, 128], P('vin', 'cell'), may hold values 0 or 1
Outputs:
- updated: bfloat16 [8, 13824, 4, 128], P('vin', 'vout', 'cell')
Inputs may be any that keep to these rules, and one draw needn't show every extreme that they name: `directions`: 1 means the component is positive, 0 negative. `cell_flags`: 1 marks a solid cell, where nothing is transported.
All inputs are finite; a program needn't handle non-finite values. No bound on the sum of `cell_flags` on one device may be relied on, other than what follows from the above.
Results may differ from a plain program's by a relative error of at most 0.023.
Values may be sent and summed in bfloat16 or wider, within the bound.
A program may use at most 128 MiB of HBM per device.

v0:
```python
import jax
import jax.numpy as jnp
from jax import lax
from jax.sharding import PartitionSpec as P

CHUNKS = 4


def from_lower(values, axis):
    ends = lax.axis_size(axis) - 1
    return lax.ppermute(values, axis, [(i, i + 1) for i in range(ends)])


def from_higher(values, axis):
    ends = lax.axis_size(axis) - 1
    return lax.ppermute(values, axis, [(i + 1, i) for i in range(ends)])


def shifted(values, step):
    edge = jnp.zeros_like(values[:, :1])
    if step > 0:
        return jnp.concatenate([edge, values[:, :-1]], axis=1)
    return jnp.concatenate([values[:, 1:], edge], axis=1)


def transport(center, neighbours, speeds, positive, fluid):
    middle = center.astype(jnp.float32)
    flux = jnp.zeros_like(middle)
    for component, (low, high) in enumerate(neighbours):
        upstream = jnp.where(positive[component][:, None], low, high).astype(jnp.float32)
        flux = flux + speeds[component][:, None] * (middle - upstream)
    return (middle - fluid[None, :] * flux).astype(jnp.bfloat16)


def on_device(distribution, collision, speeds, directions, cell_flags):
    rows = distribution.shape[2]
    velocities = collision.shape[0]
    chunk = velocities // CHUNKS
    planes = [
        lax.all_gather(distribution[:, :, row, :], "vout", axis=0, tiled=True)
        for row in range(rows)
    ]
    fluid = (1 - cell_flags[0]).astype(jnp.float32)
    relaxed = [[None] * rows for _ in range(CHUNKS)]
    for row in range(rows):
        for part in range(CHUNKS):
            block = lax.slice_in_dim(collision, part * chunk, (part + 1) * chunk, axis=0)
            partial = jnp.einsum(
                "vu,zux->zvx", block, planes[row], preferred_element_type=jnp.float32
            ).astype(jnp.bfloat16)
            relaxed[part][row] = lax.psum_scatter(partial, "vin", scatter_dimension=0, tiled=True)[
                0
            ]
    outs = []
    for part in range(CHUNKS):
        cells = relaxed[part]
        own = slice(part * chunk, (part + 1) * chunk)
        positive = directions[:, own] == 1
        pace = speeds[:, own]
        before = from_lower(cells[-1], "cell")
        after = from_higher(cells[0], "cell")
        column = [before, *cells, after]
        done = []
        for row in range(rows):
            center = cells[row]
            neighbours = (
                (shifted(center, 1), shifted(center, -1)),
                (column[row], column[row + 2]),
                (from_lower(center, "vin"), from_higher(center, "vin")),
            )
            done.append(transport(center, neighbours, pace, positive, fluid[row]))
        outs.append(jnp.stack(done, axis=1))
    return jnp.concatenate(outs, axis=0)[None]


def solution(mesh):
    return jax.shard_map(
        on_device,
        mesh=mesh,
        in_specs=(
            P("vout", "vin", "cell", None),
            P("vout", "vin"),
            P(None, "vout"),
            P(None, "vout"),
            P("vin", "cell", None),
        ),
        out_specs=P("vin", "vout", "cell", None),
        check_vma=False,
    )
```

profile of v0, /device:TPU:13, one launch (start us, length us, event | category | flops | bytes accessed | tf_op | source)
XLA Modules:
  0.0 619.9 jit_solution(6708715030905493566)
XLA Ops:
  6.5 7.7 %fusion.160 = (bf16[4,1728,1,128]{3,2,1,0:T(2,128)(2,1)S(1)}, bf16[4,1728,1,128]{3,2,1,0:T(2,128)(2,1)S(1)}) fusion(bf16[4,1728,2,128]{3,2,1,0:T(2,128)(2,1)} %param.5), kind=kLoop, calls=%fused_computation.176 | loop fusion | bytes 7077888 | tf_op jit(solution)/shard_map/slice | solution.py:40
  14.2 1.4 copy.22
  15.7 1.5 copy.21
  17.3 49.0 %all-gather.7.cloned.1.call-done = bf16[8,1728,1,128]{3,1,2,0:T(8,128)(2,1)} async-done(((bf16[4,1728,1,128]{3,1,2,0:T(8,128)(2,1)}), bf16[8,1728,1,128]{3,1,2,0:T(8,128)(2,1)}) %all-gather.7.cloned.1.call-update) | async-done | bytes 3538960 | tf_op jit(solution)/shard_map/all_gather | solution.py:40
  66.3 14.6 %fusion.56 = bf16[8,1728,128]{2,1,0:T(8,128)(2,1)} fusion(bf16[8,1728,1,128]{3,1,2,0:T(8,128)(2,1)} %all-gather.7.cloned.1.call-done, bf16[6912,1728]{0,1:T(8,128)(2,1)} %param.6), kind=kOutput, calls=%fused_computation.41 | convolution fusion | flops 6117064704 | bytes 13271040 | tf_op jit(solution)/shard_map/vu,zux->zvx/dot_general | solution.py:48
  81.0 36.3 %all-gather.5.cloned.1.call-done = bf16[8,1728,1,128]{3,1,2,0:T(8,128)(2,1)} async-done(((bf16[4,1728,1,128]{3,1,2,0:T(8,128)(2,1)}), bf16[8,1728,1,128]{3,1,2,0:T(8,128)(2,1)}) %all-gather.5.cloned.1.call-update) | async-done | bytes 3538960 | tf_op jit(solution)/shard_map/all_gather | solution.py:40
  117.2 14.6 %fusion.61 = bf16[8,1728,128]{2,1,0:T(8,128)(2,1)} fusion(bf16[8,1728,1,128]{3,1,2,0:T(8,128)(2,1)} %all-gather.5.cloned.1.call-done, bf16[6912,1728]{0,1:T(8,128)(2,1)} %param.6), kind=kOutput, calls=%fused_computation.42 | convolution fusion | flops 6117064704 | bytes 13271040 | tf_op jit(solution)/shard_map/vu,zux->zvx/dot_general | solution.py:48
  132.1 1.8 copy-done.43
  133.9 10.8 %fusion.66 = bf16[8,1728,128]{2,1,0:T(8,128)(2,1)} fusion(bf16[8,1728,1,128]{3,1,2,0:T(8,128)(2,1)S(1)} %copy-done.43, bf16[6912,1728]{0,1:T(8,128)(2,1)} %param.6), kind=kOutput, calls=%fused_computation.43 | convolution fusion | flops 6117064704 | bytes 13271040 | tf_op jit(solution)/shard_map/vu,zux->zvx/dot_general | solution.py:48
  144.8 11.5 %fusion.71 = bf16[8,1728,128]{2,1,0:T(8,128)(2,1)} fusion(bf16[8,1728,1,128]{3,1,2,0:T(8,128)(2,1)} %all-gather.5.cloned.1.call-done, bf16[6912,1728]{0,1:T(8,128)(2,1)} %param.6), kind=kOutput, calls=%fused_computation.44 | convolution fusion | flops 6117064704 | bytes 13271040 | tf_op jit(solution)/shard_map/vu,zux->zvx/dot_general | solution.py:48
  156.4 14.2 %fusion.76 = bf16[8,1728,128]{2,1,0:T(8,128)(2,1)} fusion(bf16[8,1728,1,128]{3,1,2,0:T(8,128)(2,1)S(1)} %copy-done.43, bf16[6912,1728]{0,1:T(8,128)(2,1)} %param.6), kind=kOutput, calls=%fused_computation.45 | convolution fusion | flops 6117064704 | bytes 13271040 | tf_op jit(solution)/shard_map/vu,zux->zvx/dot_general | solution.py:48
  170.9 14.7 %fusion.81 = bf16[8,1728,128]{2,1,0:T(8,128)(2,1)} fusion(bf16[8,1728,1,128]{3,1,2,0:T(8,128)(2,1)} %all-gather.5.cloned.1.call-done, bf16[6912,1728]{0,1:T(8,128)(2,1)} %param.6), kind=kOutput, calls=%fused_computation.46 | convolution fusion | flops 6117064704 | bytes 13271040 | tf_op jit(solution)/shard_map/vu,zux->zvx/dot_general | solution.py:48
  185.7 10.9 %fusion.86 = bf16[8,1728,128]{2,1,0:T(8,128)(2,1)} fusion(bf16[8,1728,1,128]{3,1,2,0:T(8,128)(2,1)S(1)} %copy-done.43, bf16[6912,1728]{0,1:T(8,128)(2,1)} %param.6), kind=kOutput, calls=%fused_computation.47 | convolution fusion | flops 6117064704 | bytes 13271040 | tf_op jit(solution)/shard_map/vu,zux->zvx/dot_general | solution.py:48
  196.6 2.0 copy-done.44
  198.6 10.9 %fusion.91 = bf16[8,1728,128]{2,1,0:T(8,128)(2,1)} fusion(bf16[8,1728,1,128]{3,1,2,0:T(8,128)(2,1)S(1)} %copy-done.44, bf16[6912,1728]{0,1:T(8,128)(2,1)} %param.6), kind=kOutput, calls=%fused_computation.48 | convolution fusion | flops 6117064704 | bytes 13271040 | tf_op jit(solution)/shard_map/vu,zux->zvx/dot_general | solution.py:48
  214.6 3.7 collective-permute-start.22
  218.4 1.9 collective-permute-start.23
  220.3 2.9 collective-permute-start.21
  223.3 3.9 collective-permute-start.19
  227.2 2.3 collective-permute-start.20
  229.5 2.2 fusion.168
  231.8 2.3 fusion.167
  234.0 26.6 %reduce-scatter.19.cloned.1.call-done = bf16[1,1728,128]{2,1,0:T(8,128)(2,1)} async-done(((bf16[8,1728,128]{2,1,0:T(8,128)(2,1)}), bf16[1,1728,128]{2,1,0:T(8,128)(2,1)}) %reduce-scatter.19.cloned.1.call-update) | async-done | bytes 442384 | tf_op jit(solution)/shard_map/reduce_scatter | solution.py:51
  260.6 2.2 fusion.166
  262.8 42.4 %reduce-scatter.17.cloned.1.call-done = bf16[1,1728,128]{2,1,0:T(8,128)(2,1)} async-done(((bf16[8,1728,128]{2,1,0:T(8,128)(2,1)}), bf16[1,1728,128]{2,1,0:T(8,128)(2,1)}) %reduce-scatter.17.cloned.1.call-update) | async-done | bytes 442384 | tf_op jit(solution)/shard_map/reduce_scatter | solution.py:51
  305.2 2.2 fusion.165
  307.5 42.4 %reduce-scatter.15.cloned.1.call-done = bf16[1,1728,128]{2,1,0:T(8,128)(2,1)} async-done(((bf16[8,1728,128]{2,1,0:T(8,128)(2,1)}), bf16[1,1728,128]{2,1,0:T(8,128)(2,1)}) %reduce-scatter.15.cloned.1.call-update) | async-done | bytes 442384 | tf_op jit(solution)/shard_map/reduce_scatter | solution.py:51
  349.9 2.3 fusion.164
  352.2 42.5 %reduce-scatter.13.cloned.1.call-done = bf16[1,1728,128]{2,1,0:T(8,128)(2,1)} async-done(((bf16[8,1728,128]{2,1,0:T(8,128)(2,1)}), bf16[1,1728,128]{2,1,0:T(8,128)(2,1)}) %reduce-scatter.13.cloned.1.call-update) | async-done | bytes 442384 | tf_op jit(solution)/shard_map/reduce_scatter | solution.py:51
  394.7 1.4 fusion.163
  396.1 43.3 %reduce-scatter.11.cloned.1.call-done = bf16[1,1728,128]{2,1,0:T(8,128)(2,1)} async-done(((bf16[8,1728,128]{2,1,0:T(8,128)(2,1)}), bf16[1,1728,128]{2,1,0:T(8,128)(2,1)}) %reduce-scatter.11.cloned.1.call-update) | async-done | bytes 442384 | tf_op jit(solution)/shard_map/reduce_scatter | solution.py:51
  439.4 1.4 fusion.162
  440.8 43.2 %reduce-scatter.9.cloned.1.call-done = bf16[1,1728,128]{2,1,0:T(8,128)(2,1)} async-done(((bf16[8,1728,128]{2,1,0:T(8,128)(2,1)}), bf16[1,1728,128]{2,1,0:T(8,128)(2,1)}) %reduce-scatter.9.cloned.1.call-update) | async-done | bytes 442384 | tf_op jit(solution)/shard_map/reduce_scatter | solution.py:51
  484.0 1.4 fusion.161
  485.5 1.3 collective-permute-start.18
  486.8 2.4 collective-permute-start.16
  489.2 1.9 collective-permute-start.17
  491.3 4.7 fusion.152
  496.0 4.3 collective-permute-start.15
  500.3 3.9 collective-permute-start.13
  504.3 1.9 collective-permute-start.14
  506.3 4.4 fusion.153
  512.0 3.6 collective-permute-start.10
  515.7 1.9 collective-permute-start.11
  517.8 2.2 fusion.154
  520.0 4.3 collective-permute-start.9
  524.4 3.9 collective-permute-start.7
  528.3 1.9 collective-permute-start.8
  530.3 2.2 fusion.155
  532.5 1.3 collective-permute-start.6
  533.8 3.6 collective-permute-start.4
  537.5 1.9 collective-permute-start.5
  539.5 2.2 fusion.156
  541.7 4.3 collective-permute-start.3
  546.1 3.9 collective-permute-start.1
  550.0 1.9 collective-permute-start.2
  551.9 2.2 fusion.157
  554.2 1.5 collective-permute-start
  555.8 2.2 fusion.158
  558.1 1.9 collective-permute-done.2
  559.9 8.1 %collective-permute-done = bf16[1728,128]{1,0:T(8,128)(2,1)S(1)} collective-permute-done((bf16[1728,128]{1,0:T(8,128)(2,1)S(1)}, bf16[1728,128]{1,0:T(8,128)(2,1)S(1)}, u32[]{:S(2)}, u32[]{:S(2)}) %collective-permute-start) | collective-permute-done | bytes 442400 | tf_op jit(solution)/shard_map/ppermute | solution.py:11
  568.1 2.2 fusion.159
  570.2 12.5 %maximum_bitcast_fusion = bf16[1,6912,2,128]{3,1,2,0:T(8,128)(2,1)S(1)} fusion(bf16[1728,1,128]{2,0,1:T(8,128)(2,1)S(1)} %fusion.152, bf16[1728,1,128]{2,0,1:T(8,128)(2,1)S(1)} %fusion.153, bf16[1728,1,128]{2,0,1:T(8,128)(2,1)S(1)} %fusion.154, bf16[1728,1,128]{2,0,1:T(8,128)(2,1)S(1)} %fusion.155, bf16[1728,1,128]{2,0,1:T(8,128)(2,1)S(1)} %fusion.156, ...), kind=kLoop, calls=%fused_computation.32 | loop fusion | flops 28311552 | bytes 7077888 | tf_op jit(solution)/shard_map/broadcast_in_dim | solution.py:73
  582.8 30.0 %copy.19 = bf16[1,6912,2,128]{3,2,1,0:T(2,128)(2,1)} copy(bf16[1,6912,2,128]{3,1,2,0:T(8,128)(2,1)S(1)} %maximum_bitcast_fusion) | data formatting | bytes 7077888 | tf_op jit(solution)/shard_map/broadcast_in_dim | solution.py:73
  (141 shorter events, 7.8 us)
Async XLA Ops:
  6.5 59.8 %all-gather.7.cloned.1.call-start = ((), (), s32[]{:S(2)}) async-start(), calls=%async_computation.17 | async-start | bytes 5308416 | tf_op jit(solution)/shard_map/all_gather | solution.py:40
  15.7 101.6 %all-gather.5.cloned.1.call-start = ((), (), s32[]{:S(2)}) async-start(), calls=%async_computation.16 | async-start | bytes 5308416 | tf_op jit(solution)/shard_map/all_gather | solution.py:40
  17.2 197.4 %reduce-scatter.23.cloned.1.call-start = ((), (), s32[]{:S(2)}) async-start(), calls=%async_computation.15 | async-start | bytes 3981312 | tf_op jit(solution)/shard_map/reduce_scatter | solution.py:51
  80.9 139.4 %reduce-scatter.21.cloned.1.call-start = ((), (), s32[]{:S(2)}) async-start(), calls=%async_computation.14 | async-start | bytes 3981312 | tf_op jit(solution)/shard_map/reduce_scatter | solution.py:51
  131.9 128.7 %reduce-scatter.19.cloned.1.call-start = ((), (), s32[]{:S(2)}) async-start(), calls=%async_computation.13 | async-start | bytes 3981312 | tf_op jit(solution)/shard_map/reduce_scatter | solution.py:51
  144.8 160.4 %reduce-scatter.17.cloned.1.call-start = ((), (), s32[]{:S(2)}) async-start(), calls=%async_computation.12 | async-start | bytes 3981312 | tf_op jit(solution)/shard_map/reduce_scatter | solution.py:51
  156.4 193.5 %reduce-scatter.15.cloned.1.call-start = ((), (), s32[]{:S(2)}) async-start(), calls=%async_computation.11 | async-start | bytes 3981312 | tf_op jit(solution)/shard_map/reduce_scatter | solution.py:51
  170.6 224.0 %reduce-scatter.13.cloned.1.call-start = ((), (), s32[]{:S(2)}) async-start(), calls=%async_computation.10 | async-start | bytes 3981312 | tf_op jit(solution)/shard_map/reduce_scatter | solution.py:51
  185.6 253.8 %reduce-scatter.11.cloned.1.call-start = ((), (), s32[]{:S(2)}) async-start(), calls=%async_computation.9 | async-start | bytes 3981312 | tf_op jit(solution)/shard_map/reduce_scatter | solution.py:51
  196.6 287.4 %reduce-scatter.9.cloned.1.call-start = ((), (), s32[]{:S(2)}) async-start(), calls=%async_computation.8 | async-start | bytes 3981312 | tf_op jit(solution)/shard_map/reduce_scatter | solution.py:51
  214.6 270.8 %collective-permute-start.22 = (bf16[1728,128]{1,0:T(8,128)(2,1)}, bf16[1728,128]{1,0:T(8,128)(2,1)}, u32[]{:S(2)}, u32[]{:S(2)}) collective-permute-start(bf16[1728,128]{1,0:T(8,128)(2,1)} %bitcast.180), channel_id=1, source_target_pairs={{0,4},{4,8},{8,12},{12,16},{16,20},{20,24},{24,28},{1,5},{5,9},{9,... | collective-permute-start | bytes 1327112 | tf_op jit(solution)/shard_map/ppermute | solution.py:11
  218.4 268.4 %collective-permute-start.23 = (bf16[1728,128]{1,0:T(8,128)(2,1)}, bf16[1728,128]{1,0:T(8,128)(2,1)}, u32[]{:S(2)}, u32[]{:S(2)}) collective-permute-start(bf16[1728,128]{1,0:T(8,128)(2,1)} %bitcast.181), channel_id=1, source_target_pairs={{4,0},{8,4},{12,8},{16,12},{20,16},{24,20},{28,24},{5,1},{9,5},{13... | collective-permute-start | bytes 1327112 | tf_op jit(solution)/shard_map/ppermute | solution.py:16
  220.3 268.9 %collective-permute-start.21 = (bf16[1728,128]{1,0:T(8,128)(2,1)}, bf16[1728,128]{1,0:T(8,128)(2,1)}, u32[]{:S(2)}, u32[]{:S(2)}) collective-permute-start(bf16[1728,128]{1,0:T(8,128)(2,1)} %bitcast.184), channel_id=1, source_target_pairs={{1,0},{3,2},{5,4},{7,6},{9,8},{11,10},{13,12},{15,14},{17,16},{19,... | collective-permute-start | bytes 1327112 | tf_op jit(solution)/shard_map/ppermute | solution.py:16
  223.3 272.7 %collective-permute-start.19 = (bf16[1728,128]{1,0:T(8,128)(2,1)}, bf16[1728,128]{1,0:T(8,128)(2,1)}, u32[]{:S(2)}, u32[]{:S(2)}) collective-permute-start(bf16[1728,128]{1,0:T(8,128)(2,1)} %bitcast.185), channel_id=1, source_target_pairs={{0,4},{4,8},{8,12},{12,16},{16,20},{20,24},{24,28},{1,5},{5,9},{9,... | collective-permute-start | bytes 1327112 | tf_op jit(solution)/shard_map/ppermute | solution.py:11
  227.2 273.1 %collective-permute-start.20 = (bf16[1728,128]{1,0:T(8,128)(2,1)}, bf16[1728,128]{1,0:T(8,128)(2,1)}, u32[]{:S(2)}, u32[]{:S(2)}) collective-permute-start(bf16[1728,128]{1,0:T(8,128)(2,1)} %bitcast.186), channel_id=1, source_target_pairs={{4,0},{8,4},{12,8},{16,12},{20,16},{24,20},{28,24},{5,1},{9,5},{13... | collective-permute-start | bytes 1327112 | tf_op jit(solution)/shard_map/ppermute | solution.py:16
  349.9 135.6 %copy-start.6 = (bf16[1,1728,128]{2,1,0:T(8,128)(2,1)S(1)}, bf16[1,1728,128]{2,1,0:T(8,128)(2,1)}, u32[]{:S(2)}) copy-start(bf16[1,1728,128]{2,1,0:T(8,128)(2,1)} %reduce-scatter.23.cloned.1.call-done) | copy-start | bytes 1327108
  349.9 136.9 %copy-start.4 = (bf16[1,1728,128]{2,1,0:T(8,128)(2,1)S(1)}, bf16[1,1728,128]{2,1,0:T(8,128)(2,1)}, u32[]{:S(2)}) copy-start(bf16[1,1728,128]{2,1,0:T(8,128)(2,1)} %reduce-scatter.19.cloned.1.call-done) | copy-start | bytes 1327108
  349.9 141.2 %copy-start.7 = (bf16[1,1728,128]{2,1,0:T(8,128)(2,1)S(1)}, bf16[1,1728,128]{2,1,0:T(8,128)(2,1)}, u32[]{:S(2)}) copy-start(bf16[1,1728,128]{2,1,0:T(8,128)(2,1)} %reduce-scatter.21.cloned.1.call-done) | copy-start | bytes 1327108
  439.4 56.6 %copy-start.5 = (bf16[1,1728,128]{2,1,0:T(8,128)(2,1)S(1)}, bf16[1,1728,128]{2,1,0:T(8,128)(2,1)}, u32[]{:S(2)}) copy-start(bf16[1,1728,128]{2,1,0:T(8,128)(2,1)} %reduce-scatter.17.cloned.1.call-done) | copy-start | bytes 1327108
  484.0 22.2 %copy-start.14 = (bf16[1728,127]{1,0:T(8,128)(2,1)S(1)}, bf16[1728,127]{1,0:T(8,128)(2,1)}, u32[]{:S(2)}) copy-start(bf16[1728,127]{1,0:T(8,128)(2,1)} %get-tuple-element.43) | copy-start | bytes 1316740
  484.0 22.2 %copy-start.15 = (bf16[1728,127]{1,0:T(8,128)(2,1)S(1)}, bf16[1728,127]{1,0:T(8,128)(2,1)}, u32[]{:S(2)}) copy-start(bf16[1728,127]{1,0:T(8,128)(2,1)} %get-tuple-element.44) | copy-start | bytes 1316740
  484.0 22.2 %copy-start.24 = (f32[1728]{0:T(1024)S(1)}, f32[1728]{0:T(1024)}, u32[]{:S(2)}) copy-start(f32[1728]{0:T(1024)} %get-tuple-element.6) | copy-start | bytes 20740
  484.0 22.2 %copy-start.25 = (f32[1728]{0:T(1024)S(1)}, f32[1728]{0:T(1024)}, u32[]{:S(2)}) copy-start(f32[1728]{0:T(1024)} %get-tuple-element.15) | copy-start | bytes 20740
  484.0 22.3 %copy-start.26 = (f32[1728]{0:T(1024)S(1)}, f32[1728]{0:T(1024)}, u32[]{:S(2)}) copy-start(f32[1728]{0:T(1024)} %get-tuple-element.16) | copy-start | bytes 20740
  484.0 22.3 %copy-start.37 = (pred[1728]{0:T(1024)(128)(4,1)S(1)}, pred[1728]{0:T(1024)(128)(4,1)}, u32[]{:S(2)}) copy-start(pred[1728]{0:T(1024)(128)(4,1)} %get-tuple-element.26) | copy-start | bytes 5188
  484.0 22.3 %copy-start.38 = (pred[1728]{0:T(1024)(128)(4,1)S(1)}, pred[1728]{0:T(1024)(128)(4,1)}, u32[]{:S(2)}) copy-start(pred[1728]{0:T(1024)(128)(4,1)} %get-tuple-element.27) | copy-start | bytes 5188
  484.0 22.3 %copy-start.39 = (pred[1728]{0:T(1024)(128)(4,1)S(1)}, pred[1728]{0:T(1024)(128)(4,1)}, u32[]{:S(2)}) copy-start(pred[1728]{0:T(1024)(128)(4,1)} %get-tuple-element.28) | copy-start | bytes 5188
  484.0 22.3 %copy-start.40 = (f32[128]{0:T(128)S(1)}, f32[128]{0:T(128)}, u32[]{:S(2)}) copy-start(f32[128]{0:T(128)} %get-tuple-element.51) | copy-start | bytes 1540
  485.5 18.8 %collective-permute-start.18 = (bf16[1728,128]{1,0:T(8,128)(2,1)S(1)}, bf16[1728,128]{1,0:T(8,128)(2,1)S(1)}, u32[]{:S(2)}, u32[]{:S(2)}) collective-permute-start(bf16[1728,128]{1,0:T(8,128)(2,1)S(1)} %bitcast.183), channel_id=1, source_target_pairs={{0,1},{2,3},{4,5},{6,7},{8,9},{10,11},{12,13},{14,15},{16,17},{18,... | collective-permute-start | bytes 1327112 | tf_op jit(solution)/shard_map/ppermute | solution.py:11
  486.8 23.9 %collective-permute-start.16 = (bf16[1728,128]{1,0:T(8,128)(2,1)S(1)}, bf16[1728,128]{1,0:T(8,128)(2,1)S(1)}, u32[]{:S(2)}, u32[]{:S(2)}) collective-permute-start(bf16[1728,128]{1,0:T(8,128)(2,1)S(1)} %bitcast.173), channel_id=1, source_target_pairs={{0,4},{4,8},{8,12},{12,16},{16,20},{20,24},{24,28},{1,5},{5,9},{9,... | collective-permute-start | bytes 1327112 | tf_op jit(solution)/shard_map/ppermute | solution.py:11
  489.2 22.8 %collective-permute-start.17 = (bf16[1728,128]{1,0:T(8,128)(2,1)S(1)}, bf16[1728,128]{1,0:T(8,128)(2,1)S(1)}, u32[]{:S(2)}, u32[]{:S(2)}) collective-permute-start(bf16[1728,128]{1,0:T(8,128)(2,1)S(1)} %bitcast.174), channel_id=1, source_target_pairs={{4,0},{8,4},{12,8},{16,12},{20,16},{24,20},{28,24},{5,1},{9,5},{13... | collective-permute-start | bytes 1327112 | tf_op jit(solution)/shard_map/ppermute | solution.py:16
  491.2 26.4 %copy-start.12 = (bf16[1728,127]{1,0:T(8,128)(2,1)S(1)}, bf16[1728,127]{1,0:T(8,128)(2,1)}, u32[]{:S(2)}) copy-start(bf16[1728,127]{1,0:T(8,128)(2,1)} %get-tuple-element.41) | copy-start | bytes 1316740
  491.2 26.4 %copy-start.13 = (bf16[1728,127]{1,0:T(8,128)(2,1)S(1)}, bf16[1728,127]{1,0:T(8,128)(2,1)}, u32[]{:S(2)}) copy-start(bf16[1728,127]{1,0:T(8,128)(2,1)} %get-tuple-element.42) | copy-start | bytes 1316740
  491.2 26.4 %copy-start.21 = (f32[1728]{0:T(1024)S(1)}, f32[1728]{0:T(1024)}, u32[]{:S(2)}) copy-start(f32[1728]{0:T(1024)} %get-tuple-element.7) | copy-start | bytes 20740
  491.2 26.4 %copy-start.22 = (f32[1728]{0:T(1024)S(1)}, f32[1728]{0:T(1024)}, u32[]{:S(2)}) copy-start(f32[1728]{0:T(1024)} %get-tuple-element.8) | copy-start | bytes 20740
  491.2 26.4 %copy-start.23 = (f32[1728]{0:T(1024)S(1)}, f32[1728]{0:T(1024)}, u32[]{:S(2)}) copy-start(f32[1728]{0:T(1024)} %get-tuple-element.9) | copy-start | bytes 20740
  491.2 26.4 %copy-start.34 = (pred[1728]{0:T(1024)(128)(4,1)S(1)}, pred[1728]{0:T(1024)(128)(4,1)}, u32[]{:S(2)}) copy-start(pred[1728]{0:T(1024)(128)(4,1)} %get-tuple-element.23) | copy-start | bytes 5188
  491.2 26.4 %copy-start.35 = (pred[1728]{0:T(1024)(128)(4,1)S(1)}, pred[1728]{0:T(1024)(128)(4,1)}, u32[]{:S(2)}) copy-start(pred[1728]{0:T(1024)(128)(4,1)} %get-tuple-element.24) | copy-start | bytes 5188
  491.2 26.4 %copy-start.36 = (pred[1728]{0:T(1024)(128)(4,1)S(1)}, pred[1728]{0:T(1024)(128)(4,1)}, u32[]{:S(2)}) copy-start(pred[1728]{0:T(1024)(128)(4,1)} %get-tuple-element.25) | copy-start | bytes 5188
  491.3 26.4 %copy-start.41 = (f32[128]{0:T(128)S(1)}, f32[128]{0:T(128)}, u32[]{:S(2)}) copy-start(f32[128]{0:T(128)} %get-tuple-element.52) | copy-start | bytes 1540
  496.0 19.7 %collective-permute-start.15 = (bf16[1728,128]{1,0:T(8,128)(2,1)S(1)}, bf16[1728,128]{1,0:T(8,128)(2,1)S(1)}, u32[]{:S(2)}, u32[]{:S(2)}) collective-permute-start(bf16[1728,128]{1,0:T(8,128)(2,1)S(1)} %bitcast.177), channel_id=1, source_target_pairs={{1,0},{3,2},{5,4},{7,6},{9,8},{11,10},{13,12},{15,14},{17,16},{19,... | collective-permute-start | bytes 1327112 | tf_op jit(solution)/shard_map/ppermute | solution.py:16
  500.3 19.7 %collective-permute-start.13 = (bf16[1728,128]{1,0:T(8,128)(2,1)S(1)}, bf16[1728,128]{1,0:T(8,128)(2,1)S(1)}, u32[]{:S(2)}, u32[]{:S(2)}) collective-permute-start(bf16[1728,128]{1,0:T(8,128)(2,1)S(1)} %bitcast.178), channel_id=1, source_target_pairs={{0,4},{4,8},{8,12},{12,16},{16,20},{20,24},{24,28},{1,5},{5,9},{9,... | collective-permute-start | bytes 1327112 | tf_op jit(solution)/shard_map/ppermute | solution.py:11
  504.3 20.1 %collective-permute-start.14 = (bf16[1728,128]{1,0:T(8,128)(2,1)S(1)}, bf16[1728,128]{1,0:T(8,128)(2,1)S(1)}, u32[]{:S(2)}, u32[]{:S(2)}) collective-permute-start(bf16[1728,128]{1,0:T(8,128)(2,1)S(1)} %bitcast.179), channel_id=1, source_target_pairs={{4,0},{8,4},{12,8},{16,12},{20,16},{24,20},{28,24},{5,1},{9,5},{13... | collective-permute-start | bytes 1327112 | tf_op jit(solution)/shard_map/ppermute | solution.py:16
  506.3 23.9 %copy-start.10 = (bf16[1728,127]{1,0:T(8,128)(2,1)S(1)}, bf16[1728,127]{1,0:T(8,128)(2,1)}, u32[]{:S(2)}) copy-start(bf16[1728,127]{1,0:T(8,128)(2,1)} %get-tuple-element.39) | copy-start | bytes 1316740
  506.3 23.9 %copy-start.11 = (bf16[1728,127]{1,0:T(8,128)(2,1)S(1)}, bf16[1728,127]{1,0:T(8,128)(2,1)}, u32[]{:S(2)}) copy-start(bf16[1728,127]{1,0:T(8,128)(2,1)} %get-tuple-element.40) | copy-start | bytes 1316740
  510.7 17.6 %collective-permute-start.12 = (bf16[1728,128]{1,0:T(8,128)(2,1)S(1)}, bf16[1728,128]{1,0:T(8,128)(2,1)S(1)}, u32[]{:S(2)}, u32[]{:S(2)}) collective-permute-start(bf16[1728,128]{1,0:T(8,128)(2,1)S(1)} %bitcast.175), channel_id=1, source_target_pairs={{0,1},{2,3},{4,5},{6,7},{8,9},{10,11},{12,13},{14,15},{16,17},{18,... | collective-permute-start | bytes 1327112 | tf_op jit(solution)/shard_map/ppermute | solution.py:11
  512.0 20.4 %collective-permute-start.10 = (bf16[1728,128]{1,0:T(8,128)(2,1)S(1)}, bf16[1728,128]{1,0:T(8,128)(2,1)S(1)}, u32[]{:S(2)}, u32[]{:S(2)}) collective-permute-start(bf16[1728,128]{1,0:T(8,128)(2,1)S(1)} %bitcast.165), channel_id=1, source_target_pairs={{0,4},{4,8},{8,12},{12,16},{16,20},{20,24},{24,28},{1,5},{5,9},{9,... | collective-permute-start | bytes 1327112 | tf_op jit(solution)/shard_map/ppermute | solution.py:11
  515.7 18.1 %collective-permute-start.11 = (bf16[1728,128]{1,0:T(8,128)(2,1)S(1)}, bf16[1728,128]{1,0:T(8,128)(2,1)S(1)}, u32[]{:S(2)}, u32[]{:S(2)}) collective-permute-start(bf16[1728,128]{1,0:T(8,128)(2,1)S(1)} %bitcast.166), channel_id=1, source_target_pairs={{4,0},{8,4},{12,8},{16,12},{20,16},{24,20},{28,24},{5,1},{9,5},{13... | collective-permute-start | bytes 1327112 | tf_op jit(solution)/shard_map/ppermute | solution.py:16
  517.7 21.7 %copy-start.8 = (bf16[1728,127]{1,0:T(8,128)(2,1)S(1)}, bf16[1728,127]{1,0:T(8,128)(2,1)}, u32[]{:S(2)}) copy-start(bf16[1728,127]{1,0:T(8,128)(2,1)} %get-tuple-element.37) | copy-start | bytes 1316740
  517.7 21.7 %copy-start.9 = (bf16[1728,127]{1,0:T(8,128)(2,1)S(1)}, bf16[1728,127]{1,0:T(8,128)(2,1)}, u32[]{:S(2)}) copy-start(bf16[1728,127]{1,0:T(8,128)(2,1)} %get-tuple-element.38) | copy-start | bytes 1316740
  517.7 21.7 %copy-start.18 = (f32[1728]{0:T(1024)S(1)}, f32[1728]{0:T(1024)}, u32[]{:S(2)}) copy-start(f32[1728]{0:T(1024)} %get-tuple-element.10) | copy-start | bytes 20740
  517.7 21.7 %copy-start.19 = (f32[1728]{0:T(1024)S(1)}, f32[1728]{0:T(1024)}, u32[]{:S(2)}) copy-start(f32[1728]{0:T(1024)} %get-tuple-element.11) | copy-start | bytes 20740
  517.8 21.7 %copy-start.20 = (f32[1728]{0:T(1024)S(1)}, f32[1728]{0:T(1024)}, u32[]{:S(2)}) copy-start(f32[1728]{0:T(1024)} %get-tuple-element.12) | copy-start | bytes 20740
  517.8 21.7 %copy-start.31 = (pred[1728]{0:T(1024)(128)(4,1)S(1)}, pred[1728]{0:T(1024)(128)(4,1)}, u32[]{:S(2)}) copy-start(pred[1728]{0:T(1024)(128)(4,1)} %get-tuple-element.20) | copy-start | bytes 5188
  520.0 17.4 %collective-permute-start.9 = (bf16[1728,128]{1,0:T(8,128)(2,1)S(1)}, bf16[1728,128]{1,0:T(8,128)(2,1)S(1)}, u32[]{:S(2)}, u32[]{:S(2)}) collective-permute-start(bf16[1728,128]{1,0:T(8,128)(2,1)S(1)} %bitcast.169), channel_id=1, source_target_pairs={{1,0},{3,2},{5,4},{7,6},{9,8},{11,10},{13,12},{15,14},{17,16},{19,... | collective-permute-start | bytes 1327112 | tf_op jit(solution)/shard_map/ppermute | solution.py:16
  524.4 17.4 %collective-permute-start.7 = (bf16[1728,128]{1,0:T(8,128)(2,1)S(1)}, bf16[1728,128]{1,0:T(8,128)(2,1)S(1)}, u32[]{:S(2)}, u32[]{:S(2)}) collective-permute-start(bf16[1728,128]{1,0:T(8,128)(2,1)S(1)} %bitcast.170), channel_id=1, source_target_pairs={{0,4},{4,8},{8,12},{12,16},{16,20},{20,24},{24,28},{1,5},{5,9},{9,... | collective-permute-start | bytes 1327112 | tf_op jit(solution)/shard_map/ppermute | solution.py:11
  528.3 17.8 %collective-permute-start.8 = (bf16[1728,128]{1,0:T(8,128)(2,1)S(1)}, bf16[1728,128]{1,0:T(8,128)(2,1)S(1)}, u32[]{:S(2)}, u32[]{:S(2)}) collective-permute-start(bf16[1728,128]{1,0:T(8,128)(2,1)S(1)} %bitcast.171), channel_id=1, source_target_pairs={{4,0},{8,4},{12,8},{16,12},{20,16},{24,20},{28,24},{5,1},{9,5},{13... | collective-permute-start | bytes 1327112 | tf_op jit(solution)/shard_map/ppermute | solution.py:16
  532.5 17.5 %collective-permute-start.6 = (bf16[1728,128]{1,0:T(8,128)(2,1)S(1)}, bf16[1728,128]{1,0:T(8,128)(2,1)S(1)}, u32[]{:S(2)}, u32[]{:S(2)}) collective-permute-start(bf16[1728,128]{1,0:T(8,128)(2,1)S(1)} %bitcast.167), channel_id=1, source_target_pairs={{0,1},{2,3},{4,5},{6,7},{8,9},{10,11},{12,13},{14,15},{16,17},{18,... | collective-permute-start | bytes 1327112 | tf_op jit(solution)/shard_map/ppermute | solution.py:11
  533.8 20.4 %collective-permute-start.4 = (bf16[1728,128]{1,0:T(8,128)(2,1)S(1)}, bf16[1728,128]{1,0:T(8,128)(2,1)S(1)}, u32[]{:S(2)}, u32[]{:S(2)}) collective-permute-start(bf16[1728,128]{1,0:T(8,128)(2,1)S(1)} %bitcast.157), channel_id=1, source_target_pairs={{0,4},{4,8},{8,12},{12,16},{16,20},{20,24},{24,28},{1,5},{5,9},{9,... | collective-permute-start | bytes 1327112 | tf_op jit(solution)/shard_map/ppermute | solution.py:11
  537.5 18.2 %collective-permute-start.5 = (bf16[1728,128]{1,0:T(8,128)(2,1)S(1)}, bf16[1728,128]{1,0:T(8,128)(2,1)S(1)}, u32[]{:S(2)}, u32[]{:S(2)}) collective-permute-start(bf16[1728,128]{1,0:T(8,128)(2,1)S(1)} %bitcast.158), channel_id=1, source_target_pairs={{4,0},{8,4},{12,8},{16,12},{20,16},{24,20},{28,24},{5,1},{9,5},{13... | collective-permute-start | bytes 1327112 | tf_op jit(solution)/shard_map/ppermute | solution.py:16
  541.7 14.1 %collective-permute-start.3 = (bf16[1728,128]{1,0:T(8,128)(2,1)S(1)}, bf16[1728,128]{1,0:T(8,128)(2,1)S(1)}, u32[]{:S(2)}, u32[]{:S(2)}) collective-permute-start(bf16[1728,128]{1,0:T(8,128)(2,1)S(1)} %bitcast.161), channel_id=1, source_target_pairs={{1,0},{3,2},{5,4},{7,6},{9,8},{11,10},{13,12},{15,14},{17,16},{19,... | collective-permute-start | bytes 1327112 | tf_op jit(solution)/shard_map/ppermute | solution.py:16
  546.1 12.0 %collective-permute-start.1 = (bf16[1728,128]{1,0:T(8,128)(2,1)S(1)}, bf16[1728,128]{1,0:T(8,128)(2,1)S(1)}, u32[]{:S(2)}, u32[]{:S(2)}) collective-permute-start(bf16[1728,128]{1,0:T(8,128)(2,1)S(1)} %bitcast.162), channel_id=1, source_target_pairs={{0,4},{4,8},{8,12},{12,16},{16,20},{20,24},{24,28},{1,5},{5,9},{9,... | collective-permute-start | bytes 1327112 | tf_op jit(solution)/shard_map/ppermute | solution.py:11
  550.0 9.9 %collective-permute-start.2 = (bf16[1728,128]{1,0:T(8,128)(2,1)S(1)}, bf16[1728,128]{1,0:T(8,128)(2,1)S(1)}, u32[]{:S(2)}, u32[]{:S(2)}) collective-permute-start(bf16[1728,128]{1,0:T(8,128)(2,1)S(1)} %bitcast.163), channel_id=1, source_target_pairs={{4,0},{8,4},{12,8},{16,12},{20,16},{24,20},{28,24},{5,1},{9,5},{13... | collective-permute-start | bytes 1327112 | tf_op jit(solution)/shard_map/ppermute | solution.py:16
  554.2 13.9 %collective-permute-start = (bf16[1728,128]{1,0:T(8,128)(2,1)S(1)}, bf16[1728,128]{1,0:T(8,128)(2,1)S(1)}, u32[]{:S(2)}, u32[]{:S(2)}) collective-permute-start(bf16[1728,128]{1,0:T(8,128)(2,1)S(1)} %bitcast.159), channel_id=1, source_target_pairs={{0,1},{2,3},{4,5},{6,7},{8,9},{10,11},{12,13},{14,15},{16,17},{18,... | collective-permute-start | bytes 1327112 | tf_op jit(solution)/shard_map/ppermute | solution.py:11
  (15 other events, 184.1 us)
Sparse Core Ops, SparseCore 0:
  15.8 50.4 all-gather.6
  67.8 49.3 all-gather.4
  119.6 42.2 reduce-scatter.22
  164.2 42.2 reduce-scatter.20
  208.7 51.8 reduce-scatter.18
  262.9 42.3 reduce-scatter.16
  307.6 42.2 reduce-scatter.14
  352.3 42.2 reduce-scatter.12
  397.0 42.2 reduce-scatter.10
  441.6 42.2 reduce-scatter.8
where the time goes:
time: 629 us; the launch traced here: 620 us
  waiting for transfers between devices  336 us (53%)
  matrix products  102 us (16%)
  starting transfers between devices  66.9 us (11%)
  local copies, waits for them, and re-layouts  65 us (10%)
  other arithmetic  34.9 us (6%)
  between operations  14.7 us (2%)
    reduce_scatter x8, waiting for transfers between devices, on_device(): lax.psum_scatter(partial, 'vin', scatter_dimension=0, tiled=True)[0]  240 us
    dot_general x8, matrix products, on_device(): jnp.einsum('vu,zux->zvx', block, planes[row], preferred_element_type=jnp....  102 us
    all_gather x2, waiting for transfers between devices, on_device(): lax.all_gather(distribution[:, :, row, :], 'vout', axis=0, tiled=True)  85.3 us
    ppermute x12, starting transfers between devices, from_lower(): return lax.ppermute(values, axis, [(i, i + 1) for i in range(ends)])  34.4 us
    ppermute x12, starting transfers between devices, from_higher(): return lax.ppermute(values, axis, [(i + 1, i) for i in range(ends)])  31.7 us
    broadcast_in_dim x1, local copies, waits for them, and re-layouts, on_device(): return jnp.concatenate(outs, axis=0)[None]  30 us
    another operation x8, other arithmetic, on_device(): outs.append(jnp.stack(done, axis=1))  22.3 us
    slice x8, local copies, waits for them, and re-layouts, shifted(): return jnp.concatenate([edge, values[:, :-1]], axis=1)  15.4 us
  transfers between devices with their start and end apart: 34, of which 11 were waited for; matrix products, arithmetic and copies ran while one was open for 23% of the time, Pallas kernels for 0%

commit v1 on v0

--- a/solution.py
+++ b/solution.py
@@ -4,6 +4,18 @@
 from jax.sharding import PartitionSpec as P
 
 CHUNKS = 4
+
+
+def collect(array, axis, dim):
+    ways, here, lap = (lax.axis_size(axis), lax.axis_index(axis), array.shape[dim])
+    line, have = (array, 1)
+    while have < ways:
+        line = jnp.concatenate(
+            [line, lax.ppermute(line, axis, [(d, (d - have) % ways) for d in range(ways)])],
+            axis=dim,
+        )
+        have = 2 * have
+    return jnp.roll(line, here * lap, axis=dim)
 
 
 def from_lower(values, axis):
@@ -36,10 +48,7 @@
     rows = distribution.shape[2]
     velocities = collision.shape[0]
     chunk = velocities // CHUNKS
-    planes = [
-        lax.all_gather(distribution[:, :, row, :], "vout", axis=0, tiled=True)
-        for row in range(rows)
-    ]
+    planes = [collect(distribution[:, :, row, :], "vout", 0) for row in range(rows)]
     fluid = (1 - cell_flags[0]).astype(jnp.float32)
     relaxed = [[None] * rows for _ in range(CHUNKS)]
     for row in range(rows):

time: 629 us -> 594 us (0.944)
  waiting for transfers between devices: 336 us -> 291 us
    all_gather x2 -> x0, waiting for transfers between devices: 85.3 us -> none  [on_device(): lax.all_gather(distribution[:, :, row, :], 'vout', axis=0, tiled=True)]
    ppermute x0 -> x2, waiting for transfers between devices: none -> 76 us  [collect(): lax.ppermute(line, axis, [(d, (d - have) % ways) for d in range(ways)])]
    reduce_scatter x8, waiting for transfers between devices: 240 us -> 205 us  [on_device(): lax.psum_scatter(partial, 'vin', scatter_dimension=0, tiled=True)[0]]
  transfers between devices with their start and end apart: 34 -> 34, of which waited for: 11 -> 10; matrix products, arithmetic and copies ran while one was open for 23% -> 22% of each run, Pallas kernels for 0% -> 0%
where the time goes in v1:
time: 594 us; the launch traced here: 586 us
  waiting for transfers between devices  291 us (49%)
  matrix products  101 us (17%)
  starting transfers between devices  71.1 us (12%)
  local copies, waits for them, and re-layouts  67.3 us (11%)
  other arithmetic  41.1 us (7%)
  between operations  14.7 us (2%)
    reduce_scatter x8, waiting for transfers between devices, on_device(): lax.psum_scatter(partial, 'vin', scatter_dimension=0, tiled=True)[0]  205 us
    dot_general x8, matrix products, on_device(): jnp.einsum('vu,zux->zvx', block, planes[row], preferred_element_type=jnp....  101 us
    ppermute x2, waiting for transfers between devices, collect(): lax.ppermute(line, axis, [(d, (d - have) % ways) for d in range(ways)])  76 us
    ppermute x12, starting transfers between devices, from_lower(): return lax.ppermute(values, axis, [(i, i + 1) for i in range(ends)])  36 us
    ppermute x12, starting transfers between devices, from_higher(): return lax.ppermute(values, axis, [(i + 1, i) for i in range(ends)])  31.7 us
    broadcast_in_dim x1, local copies, waits for them, and re-layouts, on_device(): return jnp.concatenate(outs, axis=0)[None]  30 us
    another operation x8, other arithmetic, on_device(): outs.append(jnp.stack(done, axis=1))  22.3 us
    slice x8, local copies, waits for them, and re-layouts, shifted(): return jnp.concatenate([edge, values[:, :-1]], axis=1)  15.4 us
  transfers between devices with their start and end apart: 34, of which 10 were waited for; matrix products, arithmetic and copies ran while one was open for 22% of the time, Pallas kernels for 0%

profile of v1, /device:TPU:13, one launch (start us, length us, event | category | flops | bytes accessed | tf_op | source)
XLA Modules:
  0.0 586.4 jit_solution(3161544754090907885)
XLA Ops:
  6.5 7.7 %fusion.142 = (bf16[4,1728,1,128]{3,2,1,0:T(2,128)(2,1)S(1)}, bf16[4,1728,1,128]{3,2,1,0:T(2,128)(2,1)S(1)}) fusion(bf16[4,1728,2,128]{3,2,1,0:T(2,128)(2,1)} %param.7), kind=kLoop, calls=%fused_computation.184 | loop fusion | bytes 7077888 | tf_op jit(solution)/shard_map/slice | solution.py:51
  14.2 1.4 copy.21
  16.9 38.6 %collective-permute-done.1 = bf16[4,1728,128]{2,1,0:T(8,128)(2,1)} collective-permute-done((bf16[4,1728,128]{2,1,0:T(8,128)(2,1)}, bf16[4,1728,128]{2,1,0:T(8,128)(2,1)}, u32[]{:S(2)}, u32[]{:S(2)}) %collective-permute-start.1) | collective-permute-done | bytes 1769504 | tf_op jit(solution)/shard_map/ppermute | solution.py:14
  55.4 3.8 fusion.49
  59.3 1.7 copy-done.8
  61.0 14.1 %fusion.54 = bf16[8,1728,128]{2,1,0:T(8,128)(2,1)} fusion(bf16[8,1728,128]{2,1,0:T(8,128)(2,1)S(1)} %fusion.49, bf16[6912,1728]{0,1:T(8,128)(2,1)} %param.8), kind=kOutput, calls=%fused_computation.47 | convolution fusion | flops 6117064704 | bytes 13271040 | tf_op jit(solution)/shard_map/vu,zux->zvx/dot_general | solution.py:57
  76.9 37.5 %collective-permute-done = bf16[4,1728,128]{2,1,0:T(8,128)(2,1)S(1)} collective-permute-done((bf16[4,1728,128]{2,1,0:T(8,128)(2,1)S(1)}, bf16[4,1728,128]{2,1,0:T(8,128)(2,1)S(1)}, u32[]{:S(2)}, u32[]{:S(2)}) %collective-permute-start) | collective-permute-done | bytes 1769504 | tf_op jit(solution)/shard_map/ppermute | solution.py:14
  114.3 2.4 fusion.52
  116.7 1.7 copy-done.10
  118.5 14.1 %fusion.57 = bf16[8,1728,128]{2,1,0:T(8,128)(2,1)} fusion(bf16[8,1728,128]{2,1,0:T(8,128)(2,1)S(1)} %fusion.52, bf16[6912,1728]{0,1:T(8,128)(2,1)} %param.8), kind=kOutput, calls=%fused_computation.48 | convolution fusion | flops 6117064704 | bytes 13271040 | tf_op jit(solution)/shard_map/vu,zux->zvx/dot_general | solution.py:57
  132.7 1.9 copy-done.9
  134.6 10.8 %fusion.60 = bf16[8,1728,128]{2,1,0:T(8,128)(2,1)} fusion(bf16[8,1728,128]{2,1,0:T(8,128)(2,1)S(1)} %copy-done.9, bf16[6912,1728]{0,1:T(8,128)(2,1)} %param.8), kind=kOutput, calls=%fused_computation.49 | convolution fusion | flops 6117064704 | bytes 13271040 | tf_op jit(solution)/shard_map/vu,zux->zvx/dot_general | solution.py:57
  145.7 11.5 %fusion.63 = bf16[8,1728,128]{2,1,0:T(8,128)(2,1)} fusion(bf16[8,1728,128]{2,1,0:T(8,128)(2,1)} %copy-done.10, bf16[6912,1728]{0,1:T(8,128)(2,1)} %param.8), kind=kOutput, calls=%fused_computation.50 | convolution fusion | flops 6117064704 | bytes 13271040 | tf_op jit(solution)/shard_map/vu,zux->zvx/dot_general | solution.py:57
  157.2 14.2 %fusion.66 = bf16[8,1728,128]{2,1,0:T(8,128)(2,1)} fusion(bf16[8,1728,128]{2,1,0:T(8,128)(2,1)S(1)} %copy-done.9, bf16[6912,1728]{0,1:T(8,128)(2,1)} %param.8), kind=kOutput, calls=%fused_computation.51 | convolution fusion | flops 6117064704 | bytes 13271040 | tf_op jit(solution)/shard_map/vu,zux->zvx/dot_general | solution.py:57
  171.8 14.7 %fusion.69 = bf16[8,1728,128]{2,1,0:T(8,128)(2,1)} fusion(bf16[8,1728,128]{2,1,0:T(8,128)(2,1)} %copy-done.10, bf16[6912,1728]{0,1:T(8,128)(2,1)} %param.8), kind=kOutput, calls=%fused_computation.52 | convolution fusion | flops 6117064704 | bytes 13271040 | tf_op jit(solution)/shard_map/vu,zux->zvx/dot_general | solution.py:57
  186.6 10.9 %fusion.72 = bf16[8,1728,128]{2,1,0:T(8,128)(2,1)} fusion(bf16[8,1728,128]{2,1,0:T(8,128)(2,1)S(1)} %copy-done.9, bf16[6912,1728]{0,1:T(8,128)(2,1)} %param.8), kind=kOutput, calls=%fused_computation.53 | convolution fusion | flops 6117064704 | bytes 13271040 | tf_op jit(solution)/shard_map/vu,zux->zvx/dot_general | solution.py:57
  197.6 2.0 copy-done.11
  199.6 10.9 %fusion.75 = bf16[8,1728,128]{2,1,0:T(8,128)(2,1)} fusion(bf16[8,1728,128]{2,1,0:T(8,128)(2,1)S(1)} %copy-done.11, bf16[6912,1728]{0,1:T(8,128)(2,1)} %param.8), kind=kOutput, calls=%fused_computation.54 | convolution fusion | flops 6117064704 | bytes 13271040 | tf_op jit(solution)/shard_map/vu,zux->zvx/dot_general | solution.py:57
  215.6 5.4 collective-permute-start.24
  221.0 1.9 collective-permute-start.25
  222.9 2.9 collective-permute-start.23
  225.9 3.9 collective-permute-start.21
  229.8 2.4 collective-permute-start.22
  232.2 2.2 fusion.150
  234.4 2.3 fusion.149
  236.7 2.2 fusion.148
  238.9 33.1 %reduce-scatter.17.cloned.1.call-done = bf16[1,1728,128]{2,1,0:T(8,128)(2,1)} async-done(((bf16[8,1728,128]{2,1,0:T(8,128)(2,1)}), bf16[1,1728,128]{2,1,0:T(8,128)(2,1)}) %reduce-scatter.17.cloned.1.call-update) | async-done | bytes 442384 | tf_op jit(solution)/shard_map/reduce_scatter | solution.py:60
  272.0 2.2 fusion.147
  274.2 42.3 %reduce-scatter.15.cloned.1.call-done = bf16[1,1728,128]{2,1,0:T(8,128)(2,1)} async-done(((bf16[8,1728,128]{2,1,0:T(8,128)(2,1)}), bf16[1,1728,128]{2,1,0:T(8,128)(2,1)}) %reduce-scatter.15.cloned.1.call-update) | async-done | bytes 442384 | tf_op jit(solution)/shard_map/reduce_scatter | solution.py:60
  316.5 2.3 fusion.146
  318.9 42.3 %reduce-scatter.13.cloned.1.call-done = bf16[1,1728,128]{2,1,0:T(8,128)(2,1)} async-done(((bf16[8,1728,128]{2,1,0:T(8,128)(2,1)}), bf16[1,1728,128]{2,1,0:T(8,128)(2,1)}) %reduce-scatter.13.cloned.1.call-update) | async-done | bytes 442384 | tf_op jit(solution)/shard_map/reduce_scatter | solution.py:60
  361.2 1.3 fusion.145
  362.5 43.4 %reduce-scatter.11.cloned.1.call-done = bf16[1,1728,128]{2,1,0:T(8,128)(2,1)} async-done(((bf16[8,1728,128]{2,1,0:T(8,128)(2,1)}), bf16[1,1728,128]{2,1,0:T(8,128)(2,1)}) %reduce-scatter.11.cloned.1.call-update) | async-done | bytes 442384 | tf_op jit(solution)/shard_map/reduce_scatter | solution.py:60
  405.9 1.4 fusion.144
  407.3 43.4 %reduce-scatter.9.cloned.1.call-done = bf16[1,1728,128]{2,1,0:T(8,128)(2,1)} async-done(((bf16[8,1728,128]{2,1,0:T(8,128)(2,1)}), bf16[1,1728,128]{2,1,0:T(8,128)(2,1)}) %reduce-scatter.9.cloned.1.call-update) | async-done | bytes 442384 | tf_op jit(solution)/shard_map/reduce_scatter | solution.py:60
  450.8 1.4 fusion.143
  453.5 2.3 collective-permute-start.18
  455.8 2.0 collective-permute-start.19
  458.0 4.7 fusion.134
  462.7 4.2 collective-permute-start.17
  467.0 3.9 collective-permute-start.15
  470.9 1.9 collective-permute-start.16
  473.0 4.4 fusion.135
  478.6 3.6 collective-permute-start.12
  482.3 1.9 collective-permute-start.13
  484.4 2.2 fusion.136
  486.6 4.3 collective-permute-start.11
  491.0 3.9 collective-permute-start.9
  494.9 1.9 collective-permute-start.10
  496.9 2.2 fusion.137
  500.4 3.6 collective-permute-start.6
  504.1 1.9 collective-permute-start.7
  506.1 2.2 fusion.138
  508.4 4.3 collective-permute-start.5
  512.7 3.9 collective-permute-start.3
  516.6 1.9 collective-permute-start.4
  518.6 2.2 fusion.139
  520.8 1.5 collective-permute-start.2
  522.4 2.2 fusion.140
  524.6 2.0 collective-permute-done.4
  526.6 8.0 %collective-permute-done.2 = bf16[1728,128]{1,0:T(8,128)(2,1)S(1)} collective-permute-done((bf16[1728,128]{1,0:T(8,128)(2,1)S(1)}, bf16[1728,128]{1,0:T(8,128)(2,1)S(1)}, u32[]{:S(2)}, u32[]{:S(2)}) %collective-permute-start.2) | collective-permute-done | bytes 442400 | tf_op jit(solution)/shard_map/ppermute | solution.py:23
  534.6 2.2 fusion.141
  536.8 12.5 %maximum_bitcast_fusion = bf16[1,6912,2,128]{3,1,2,0:T(8,128)(2,1)S(1)} fusion(bf16[1728,1,128]{2,0,1:T(8,128)(2,1)S(1)} %fusion.134, bf16[1728,1,128]{2,0,1:T(8,128)(2,1)S(1)} %fusion.135, bf16[1728,1,128]{2,0,1:T(8,128)(2,1)S(1)} %fusion.136, bf16[1728,1,128]{2,0,1:T(8,128)(2,1)S(1)} %fusion.137, bf16[1728,1,128]{2,0,1:T(8,128)(2,1)S(1)} %fusion.138, ...), kind=kLoop, calls=%fused_computation.46 | loop fusion | flops 28311552 | bytes 7077888 | tf_op jit(solution)/shard_map/broadcast_in_dim | solution.py:82
  549.3 30.0 %copy.12 = bf16[1,6912,2,128]{3,2,1,0:T(2,128)(2,1)} copy(bf16[1,6912,2,128]{3,1,2,0:T(8,128)(2,1)S(1)} %maximum_bitcast_fusion) | data formatting | bytes 7077888 | tf_op jit(solution)/shard_map/broadcast_in_dim | solution.py:82
  (145 shorter events, 13.1 us)
Async XLA Ops:
  6.5 209.1 %reduce-scatter.23.cloned.1.call-start = ((), (), s32[]{:S(2)}) async-start(), calls=%async_computation.15 | async-start | bytes 3981312 | tf_op jit(solution)/shard_map/reduce_scatter | solution.py:60
  15.7 39.8 %collective-permute-start.1 = (bf16[4,1728,128]{2,1,0:T(8,128)(2,1)}, bf16[4,1728,128]{2,1,0:T(8,128)(2,1)}, u32[]{:S(2)}, u32[]{:S(2)}) collective-permute-start(bf16[4,1728,128]{2,1,0:T(8,128)(2,1)} %bitcast.134), channel_id=1, source_target_pairs={{0,2},{2,0},{1,3},{3,1},{4,6},{6,4},{5,7},{7,5},{8,10},{10,8},{9,1... | collective-permute-start | bytes 5308424 | tf_op jit(solution)/shard_map/ppermute | solution.py:14
  75.1 147.8 %reduce-scatter.21.cloned.1.call-start = ((), (), s32[]{:S(2)}) async-start(), calls=%async_computation.14 | async-start | bytes 3981312 | tf_op jit(solution)/shard_map/reduce_scatter | solution.py:60
  75.6 38.7 %collective-permute-start = (bf16[4,1728,128]{2,1,0:T(8,128)(2,1)S(1)}, bf16[4,1728,128]{2,1,0:T(8,128)(2,1)S(1)}, u32[]{:S(2)}, u32[]{:S(2)}) collective-permute-start(bf16[4,1728,128]{2,1,0:T(8,128)(2,1)S(1)} %bitcast.136), channel_id=1, source_target_pairs={{0,2},{2,0},{1,3},{3,1},{4,6},{6,4},{5,7},{7,5},{8,10},{10,8},{9,1... | collective-permute-start | bytes 5308424 | tf_op jit(solution)/shard_map/ppermute | solution.py:14
  132.6 104.0 %reduce-scatter.19.cloned.1.call-start = ((), (), s32[]{:S(2)}) async-start(), calls=%async_computation.13 | async-start | bytes 3981312 | tf_op jit(solution)/shard_map/reduce_scatter | solution.py:60
  145.4 126.6 %reduce-scatter.17.cloned.1.call-start = ((), (), s32[]{:S(2)}) async-start(), calls=%async_computation.12 | async-start | bytes 3981312 | tf_op jit(solution)/shard_map/reduce_scatter | solution.py:60
  157.2 159.3 %reduce-scatter.15.cloned.1.call-start = ((), (), s32[]{:S(2)}) async-start(), calls=%async_computation.11 | async-start | bytes 3981312 | tf_op jit(solution)/shard_map/reduce_scatter | solution.py:60
  171.5 189.7 %reduce-scatter.13.cloned.1.call-start = ((), (), s32[]{:S(2)}) async-start(), calls=%async_computation.10 | async-start | bytes 3981312 | tf_op jit(solution)/shard_map/reduce_scatter | solution.py:60
  186.5 219.4 %reduce-scatter.11.cloned.1.call-start = ((), (), s32[]{:S(2)}) async-start(), calls=%async_computation.9 | async-start | bytes 3981312 | tf_op jit(solution)/shard_map/reduce_scatter | solution.py:60
  197.6 253.2 %reduce-scatter.9.cloned.1.call-start = ((), (), s32[]{:S(2)}) async-start(), calls=%async_computation.8 | async-start | bytes 3981312 | tf_op jit(solution)/shard_map/reduce_scatter | solution.py:60
  215.6 236.6 %collective-permute-start.24 = (bf16[1728,128]{1,0:T(8,128)(2,1)}, bf16[1728,128]{1,0:T(8,128)(2,1)}, u32[]{:S(2)}, u32[]{:S(2)}) collective-permute-start(bf16[1728,128]{1,0:T(8,128)(2,1)} %bitcast.162), channel_id=1, source_target_pairs={{0,4},{4,8},{8,12},{12,16},{16,20},{20,24},{24,28},{1,5},{5,9},{9,... | collective-permute-start | bytes 1327112 | tf_op jit(solution)/shard_map/ppermute | solution.py:23
  221.0 232.5 %collective-permute-start.25 = (bf16[1728,128]{1,0:T(8,128)(2,1)}, bf16[1728,128]{1,0:T(8,128)(2,1)}, u32[]{:S(2)}, u32[]{:S(2)}) collective-permute-start(bf16[1728,128]{1,0:T(8,128)(2,1)} %bitcast.163), channel_id=1, source_target_pairs={{4,0},{8,4},{12,8},{16,12},{20,16},{24,20},{28,24},{5,1},{9,5},{13... | collective-permute-start | bytes 1327112 | tf_op jit(solution)/shard_map/ppermute | solution.py:28
  222.9 232.9 %collective-permute-start.23 = (bf16[1728,128]{1,0:T(8,128)(2,1)}, bf16[1728,128]{1,0:T(8,128)(2,1)}, u32[]{:S(2)}, u32[]{:S(2)}) collective-permute-start(bf16[1728,128]{1,0:T(8,128)(2,1)} %bitcast.166), channel_id=1, source_target_pairs={{1,0},{3,2},{5,4},{7,6},{9,8},{11,10},{13,12},{15,14},{17,16},{19,... | collective-permute-start | bytes 1327112 | tf_op jit(solution)/shard_map/ppermute | solution.py:28
  225.9 236.8 %collective-permute-start.21 = (bf16[1728,128]{1,0:T(8,128)(2,1)}, bf16[1728,128]{1,0:T(8,128)(2,1)}, u32[]{:S(2)}, u32[]{:S(2)}) collective-permute-start(bf16[1728,128]{1,0:T(8,128)(2,1)} %bitcast.167), channel_id=1, source_target_pairs={{0,4},{4,8},{8,12},{12,16},{16,20},{20,24},{24,28},{1,5},{5,9},{9,... | collective-permute-start | bytes 1327112 | tf_op jit(solution)/shard_map/ppermute | solution.py:23
  229.8 237.2 %collective-permute-start.22 = (bf16[1728,128]{1,0:T(8,128)(2,1)}, bf16[1728,128]{1,0:T(8,128)(2,1)}, u32[]{:S(2)}, u32[]{:S(2)}) collective-permute-start(bf16[1728,128]{1,0:T(8,128)(2,1)} %bitcast.168), channel_id=1, source_target_pairs={{4,0},{8,4},{12,8},{16,12},{20,16},{24,20},{28,24},{5,1},{9,5},{13... | collective-permute-start | bytes 1327112 | tf_op jit(solution)/shard_map/ppermute | solution.py:28
  316.5 135.6 %copy-start.6 = (bf16[1,1728,128]{2,1,0:T(8,128)(2,1)S(1)}, bf16[1,1728,128]{2,1,0:T(8,128)(2,1)}, u32[]{:S(2)}) copy-start(bf16[1,1728,128]{2,1,0:T(8,128)(2,1)} %reduce-scatter.23.cloned.1.call-done) | copy-start | bytes 1327108
  316.5 137.0 %copy-start.4 = (bf16[1,1728,128]{2,1,0:T(8,128)(2,1)S(1)}, bf16[1,1728,128]{2,1,0:T(8,128)(2,1)}, u32[]{:S(2)}) copy-start(bf16[1,1728,128]{2,1,0:T(8,128)(2,1)} %reduce-scatter.19.cloned.1.call-done) | copy-start | bytes 1327108
  316.5 141.3 %copy-start.7 = (bf16[1,1728,128]{2,1,0:T(8,128)(2,1)S(1)}, bf16[1,1728,128]{2,1,0:T(8,128)(2,1)}, u32[]{:S(2)}) copy-start(bf16[1,1728,128]{2,1,0:T(8,128)(2,1)} %reduce-scatter.21.cloned.1.call-done) | copy-start | bytes 1327108
  405.9 56.8 %copy-start.5 = (bf16[1,1728,128]{2,1,0:T(8,128)(2,1)S(1)}, bf16[1,1728,128]{2,1,0:T(8,128)(2,1)}, u32[]{:S(2)}) copy-start(bf16[1,1728,128]{2,1,0:T(8,128)(2,1)} %reduce-scatter.17.cloned.1.call-done) | copy-start | bytes 1327108
  450.7 22.1 %copy-start.18 = (bf16[1728,127]{1,0:T(8,128)(2,1)S(1)}, bf16[1728,127]{1,0:T(8,128)(2,1)}, u32[]{:S(2)}) copy-start(bf16[1728,127]{1,0:T(8,128)(2,1)} %get-tuple-element.44) | copy-start | bytes 1316740
  450.7 22.1 %copy-start.19 = (bf16[1728,127]{1,0:T(8,128)(2,1)S(1)}, bf16[1728,127]{1,0:T(8,128)(2,1)}, u32[]{:S(2)}) copy-start(bf16[1728,127]{1,0:T(8,128)(2,1)} %get-tuple-element.45) | copy-start | bytes 1316740
  450.7 22.1 %copy-start.28 = (f32[1728]{0:T(1024)S(1)}, f32[1728]{0:T(1024)}, u32[]{:S(2)}) copy-start(f32[1728]{0:T(1024)} %get-tuple-element.7) | copy-start | bytes 20740
  450.7 22.2 %copy-start.29 = (f32[1728]{0:T(1024)S(1)}, f32[1728]{0:T(1024)}, u32[]{:S(2)}) copy-start(f32[1728]{0:T(1024)} %get-tuple-element.16) | copy-start | bytes 20740
  450.7 22.2 %copy-start.30 = (f32[1728]{0:T(1024)S(1)}, f32[1728]{0:T(1024)}, u32[]{:S(2)}) copy-start(f32[1728]{0:T(1024)} %get-tuple-element.17) | copy-start | bytes 20740
  450.7 22.2 %copy-start.41 = (pred[1728]{0:T(1024)(128)(4,1)S(1)}, pred[1728]{0:T(1024)(128)(4,1)}, u32[]{:S(2)}) copy-start(pred[1728]{0:T(1024)(128)(4,1)} %get-tuple-element.27) | copy-start | bytes 5188
  450.7 22.2 %copy-start.42 = (pred[1728]{0:T(1024)(128)(4,1)S(1)}, pred[1728]{0:T(1024)(128)(4,1)}, u32[]{:S(2)}) copy-start(pred[1728]{0:T(1024)(128)(4,1)} %get-tuple-element.28) | copy-start | bytes 5188
  450.7 22.2 %copy-start.43 = (pred[1728]{0:T(1024)(128)(4,1)S(1)}, pred[1728]{0:T(1024)(128)(4,1)}, u32[]{:S(2)}) copy-start(pred[1728]{0:T(1024)(128)(4,1)} %get-tuple-element.29) | copy-start | bytes 5188
  450.7 22.2 %copy-start.44 = (f32[128]{0:T(128)S(1)}, f32[128]{0:T(128)}, u32[]{:S(2)}) copy-start(f32[128]{0:T(128)} %get-tuple-element.52) | copy-start | bytes 1540
  452.2 18.7 %collective-permute-start.20 = (bf16[1728,128]{1,0:T(8,128)(2,1)S(1)}, bf16[1728,128]{1,0:T(8,128)(2,1)S(1)}, u32[]{:S(2)}, u32[]{:S(2)}) collective-permute-start(bf16[1728,128]{1,0:T(8,128)(2,1)S(1)} %bitcast.165), channel_id=1, source_target_pairs={{0,1},{2,3},{4,5},{6,7},{8,9},{10,11},{12,13},{14,15},{16,17},{18,... | collective-permute-start | bytes 1327112 | tf_op jit(solution)/shard_map/ppermute | solution.py:23
  453.5 23.8 %collective-permute-start.18 = (bf16[1728,128]{1,0:T(8,128)(2,1)S(1)}, bf16[1728,128]{1,0:T(8,128)(2,1)S(1)}, u32[]{:S(2)}, u32[]{:S(2)}) collective-permute-start(bf16[1728,128]{1,0:T(8,128)(2,1)S(1)} %bitcast.155), channel_id=1, source_target_pairs={{0,4},{4,8},{8,12},{12,16},{16,20},{20,24},{24,28},{1,5},{5,9},{9,... | collective-permute-start | bytes 1327112 | tf_op jit(solution)/shard_map/ppermute | solution.py:23
  455.8 22.8 %collective-permute-start.19 = (bf16[1728,128]{1,0:T(8,128)(2,1)S(1)}, bf16[1728,128]{1,0:T(8,128)(2,1)S(1)}, u32[]{:S(2)}, u32[]{:S(2)}) collective-permute-start(bf16[1728,128]{1,0:T(8,128)(2,1)S(1)} %bitcast.156), channel_id=1, source_target_pairs={{4,0},{8,4},{12,8},{16,12},{20,16},{24,20},{28,24},{5,1},{9,5},{13... | collective-permute-start | bytes 1327112 | tf_op jit(solution)/shard_map/ppermute | solution.py:28
  457.9 26.4 %copy-start.16 = (bf16[1728,127]{1,0:T(8,128)(2,1)S(1)}, bf16[1728,127]{1,0:T(8,128)(2,1)}, u32[]{:S(2)}) copy-start(bf16[1728,127]{1,0:T(8,128)(2,1)} %get-tuple-element.42) | copy-start | bytes 1316740
  457.9 26.4 %copy-start.17 = (bf16[1728,127]{1,0:T(8,128)(2,1)S(1)}, bf16[1728,127]{1,0:T(8,128)(2,1)}, u32[]{:S(2)}) copy-start(bf16[1728,127]{1,0:T(8,128)(2,1)} %get-tuple-element.43) | copy-start | bytes 1316740
  457.9 26.4 %copy-start.25 = (f32[1728]{0:T(1024)S(1)}, f32[1728]{0:T(1024)}, u32[]{:S(2)}) copy-start(f32[1728]{0:T(1024)} %get-tuple-element.8) | copy-start | bytes 20740
  457.9 26.4 %copy-start.26 = (f32[1728]{0:T(1024)S(1)}, f32[1728]{0:T(1024)}, u32[]{:S(2)}) copy-start(f32[1728]{0:T(1024)} %get-tuple-element.9) | copy-start | bytes 20740
  457.9 26.4 %copy-start.27 = (f32[1728]{0:T(1024)S(1)}, f32[1728]{0:T(1024)}, u32[]{:S(2)}) copy-start(f32[1728]{0:T(1024)} %get-tuple-element.10) | copy-start | bytes 20740
  457.9 26.4 %copy-start.38 = (pred[1728]{0:T(1024)(128)(4,1)S(1)}, pred[1728]{0:T(1024)(128)(4,1)}, u32[]{:S(2)}) copy-start(pred[1728]{0:T(1024)(128)(4,1)} %get-tuple-element.24) | copy-start | bytes 5188
  457.9 26.4 %copy-start.39 = (pred[1728]{0:T(1024)(128)(4,1)S(1)}, pred[1728]{0:T(1024)(128)(4,1)}, u32[]{:S(2)}) copy-start(pred[1728]{0:T(1024)(128)(4,1)} %get-tuple-element.25) | copy-start | bytes 5188
  457.9 26.4 %copy-start.40 = (pred[1728]{0:T(1024)(128)(4,1)S(1)}, pred[1728]{0:T(1024)(128)(4,1)}, u32[]{:S(2)}) copy-start(pred[1728]{0:T(1024)(128)(4,1)} %get-tuple-element.26) | copy-start | bytes 5188
  458.0 26.4 %copy-start.45 = (f32[128]{0:T(128)S(1)}, f32[128]{0:T(128)}, u32[]{:S(2)}) copy-start(f32[128]{0:T(128)} %get-tuple-element.53) | copy-start | bytes 1540
  462.7 19.6 %collective-permute-start.17 = (bf16[1728,128]{1,0:T(8,128)(2,1)S(1)}, bf16[1728,128]{1,0:T(8,128)(2,1)S(1)}, u32[]{:S(2)}, u32[]{:S(2)}) collective-permute-start(bf16[1728,128]{1,0:T(8,128)(2,1)S(1)} %bitcast.159), channel_id=1, source_target_pairs={{1,0},{3,2},{5,4},{7,6},{9,8},{11,10},{13,12},{15,14},{17,16},{19,... | collective-permute-start | bytes 1327112 | tf_op jit(solution)/shard_map/ppermute | solution.py:28
  467.0 19.7 %collective-permute-start.15 = (bf16[1728,128]{1,0:T(8,128)(2,1)S(1)}, bf16[1728,128]{1,0:T(8,128)(2,1)S(1)}, u32[]{:S(2)}, u32[]{:S(2)}) collective-permute-start(bf16[1728,128]{1,0:T(8,128)(2,1)S(1)} %bitcast.160), channel_id=1, source_target_pairs={{0,4},{4,8},{8,12},{12,16},{16,20},{20,24},{24,28},{1,5},{5,9},{9,... | collective-permute-start | bytes 1327112 | tf_op jit(solution)/shard_map/ppermute | solution.py:23
  470.9 20.1 %collective-permute-start.16 = (bf16[1728,128]{1,0:T(8,128)(2,1)S(1)}, bf16[1728,128]{1,0:T(8,128)(2,1)S(1)}, u32[]{:S(2)}, u32[]{:S(2)}) collective-permute-start(bf16[1728,128]{1,0:T(8,128)(2,1)S(1)} %bitcast.161), channel_id=1, source_target_pairs={{4,0},{8,4},{12,8},{16,12},{20,16},{24,20},{28,24},{5,1},{9,5},{13... | collective-permute-start | bytes 1327112 | tf_op jit(solution)/shard_map/ppermute | solution.py:28
  472.9 23.9 %copy-start.14 = (bf16[1728,127]{1,0:T(8,128)(2,1)S(1)}, bf16[1728,127]{1,0:T(8,128)(2,1)}, u32[]{:S(2)}) copy-start(bf16[1728,127]{1,0:T(8,128)(2,1)} %get-tuple-element.40) | copy-start | bytes 1316740
  472.9 23.9 %copy-start.15 = (bf16[1728,127]{1,0:T(8,128)(2,1)S(1)}, bf16[1728,127]{1,0:T(8,128)(2,1)}, u32[]{:S(2)}) copy-start(bf16[1728,127]{1,0:T(8,128)(2,1)} %get-tuple-element.41) | copy-start | bytes 1316740
  477.3 17.6 %collective-permute-start.14 = (bf16[1728,128]{1,0:T(8,128)(2,1)S(1)}, bf16[1728,128]{1,0:T(8,128)(2,1)S(1)}, u32[]{:S(2)}, u32[]{:S(2)}) collective-permute-start(bf16[1728,128]{1,0:T(8,128)(2,1)S(1)} %bitcast.157), channel_id=1, source_target_pairs={{0,1},{2,3},{4,5},{6,7},{8,9},{10,11},{12,13},{14,15},{16,17},{18,... | collective-permute-start | bytes 1327112 | tf_op jit(solution)/shard_map/ppermute | solution.py:23
  478.6 20.4 %collective-permute-start.12 = (bf16[1728,128]{1,0:T(8,128)(2,1)S(1)}, bf16[1728,128]{1,0:T(8,128)(2,1)S(1)}, u32[]{:S(2)}, u32[]{:S(2)}) collective-permute-start(bf16[1728,128]{1,0:T(8,128)(2,1)S(1)} %bitcast.147), channel_id=1, source_target_pairs={{0,4},{4,8},{8,12},{12,16},{16,20},{20,24},{24,28},{1,5},{5,9},{9,... | collective-permute-start | bytes 1327112 | tf_op jit(solution)/shard_map/ppermute | solution.py:23
  482.3 18.1 %collective-permute-start.13 = (bf16[1728,128]{1,0:T(8,128)(2,1)S(1)}, bf16[1728,128]{1,0:T(8,128)(2,1)S(1)}, u32[]{:S(2)}, u32[]{:S(2)}) collective-permute-start(bf16[1728,128]{1,0:T(8,128)(2,1)S(1)} %bitcast.148), channel_id=1, source_target_pairs={{4,0},{8,4},{12,8},{16,12},{20,16},{24,20},{28,24},{5,1},{9,5},{13... | collective-permute-start | bytes 1327112 | tf_op jit(solution)/shard_map/ppermute | solution.py:28
  484.3 21.7 %copy-start.12 = (bf16[1728,127]{1,0:T(8,128)(2,1)S(1)}, bf16[1728,127]{1,0:T(8,128)(2,1)}, u32[]{:S(2)}) copy-start(bf16[1728,127]{1,0:T(8,128)(2,1)} %get-tuple-element.38) | copy-start | bytes 1316740
  484.3 21.7 %copy-start.13 = (bf16[1728,127]{1,0:T(8,128)(2,1)S(1)}, bf16[1728,127]{1,0:T(8,128)(2,1)}, u32[]{:S(2)}) copy-start(bf16[1728,127]{1,0:T(8,128)(2,1)} %get-tuple-element.39) | copy-start | bytes 1316740
  484.4 21.7 %copy-start.22 = (f32[1728]{0:T(1024)S(1)}, f32[1728]{0:T(1024)}, u32[]{:S(2)}) copy-start(f32[1728]{0:T(1024)} %get-tuple-element.11) | copy-start | bytes 20740
  484.4 21.7 %copy-start.23 = (f32[1728]{0:T(1024)S(1)}, f32[1728]{0:T(1024)}, u32[]{:S(2)}) copy-start(f32[1728]{0:T(1024)} %get-tuple-element.12) | copy-start | bytes 20740
  484.4 21.7 %copy-start.24 = (f32[1728]{0:T(1024)S(1)}, f32[1728]{0:T(1024)}, u32[]{:S(2)}) copy-start(f32[1728]{0:T(1024)} %get-tuple-element.13) | copy-start | bytes 20740
  484.4 21.7 %copy-start.35 = (pred[1728]{0:T(1024)(128)(4,1)S(1)}, pred[1728]{0:T(1024)(128)(4,1)}, u32[]{:S(2)}) copy-start(pred[1728]{0:T(1024)(128)(4,1)} %get-tuple-element.21) | copy-start | bytes 5188
  486.6 17.4 %collective-permute-start.11 = (bf16[1728,128]{1,0:T(8,128)(2,1)S(1)}, bf16[1728,128]{1,0:T(8,128)(2,1)S(1)}, u32[]{:S(2)}, u32[]{:S(2)}) collective-permute-start(bf16[1728,128]{1,0:T(8,128)(2,1)S(1)} %bitcast.151), channel_id=1, source_target_pairs={{1,0},{3,2},{5,4},{7,6},{9,8},{11,10},{13,12},{15,14},{17,16},{19,... | collective-permute-start | bytes 1327112 | tf_op jit(solution)/shard_map/ppermute | solution.py:28
  491.0 17.4 %collective-permute-start.9 = (bf16[1728,128]{1,0:T(8,128)(2,1)S(1)}, bf16[1728,128]{1,0:T(8,128)(2,1)S(1)}, u32[]{:S(2)}, u32[]{:S(2)}) collective-permute-start(bf16[1728,128]{1,0:T(8,128)(2,1)S(1)} %bitcast.152), channel_id=1, source_target_pairs={{0,4},{4,8},{8,12},{12,16},{16,20},{20,24},{24,28},{1,5},{5,9},{9,... | collective-permute-start | bytes 1327112 | tf_op jit(solution)/shard_map/ppermute | solution.py:23
  494.9 17.8 %collective-permute-start.10 = (bf16[1728,128]{1,0:T(8,128)(2,1)S(1)}, bf16[1728,128]{1,0:T(8,128)(2,1)S(1)}, u32[]{:S(2)}, u32[]{:S(2)}) collective-permute-start(bf16[1728,128]{1,0:T(8,128)(2,1)S(1)} %bitcast.153), channel_id=1, source_target_pairs={{4,0},{8,4},{12,8},{16,12},{20,16},{24,20},{28,24},{5,1},{9,5},{13... | collective-permute-start | bytes 1327112 | tf_op jit(solution)/shard_map/ppermute | solution.py:28
  499.1 17.5 %collective-permute-start.8 = (bf16[1728,128]{1,0:T(8,128)(2,1)S(1)}, bf16[1728,128]{1,0:T(8,128)(2,1)S(1)}, u32[]{:S(2)}, u32[]{:S(2)}) collective-permute-start(bf16[1728,128]{1,0:T(8,128)(2,1)S(1)} %bitcast.149), channel_id=1, source_target_pairs={{0,1},{2,3},{4,5},{6,7},{8,9},{10,11},{12,13},{14,15},{16,17},{18,... | collective-permute-start | bytes 1327112 | tf_op jit(solution)/shard_map/ppermute | solution.py:23
  500.4 20.4 %collective-permute-start.6 = (bf16[1728,128]{1,0:T(8,128)(2,1)S(1)}, bf16[1728,128]{1,0:T(8,128)(2,1)S(1)}, u32[]{:S(2)}, u32[]{:S(2)}) collective-permute-start(bf16[1728,128]{1,0:T(8,128)(2,1)S(1)} %bitcast.139), channel_id=1, source_target_pairs={{0,4},{4,8},{8,12},{12,16},{16,20},{20,24},{24,28},{1,5},{5,9},{9,... | collective-permute-start | bytes 1327112 | tf_op jit(solution)/shard_map/ppermute | solution.py:23
  504.1 18.2 %collective-permute-start.7 = (bf16[1728,128]{1,0:T(8,128)(2,1)S(1)}, bf16[1728,128]{1,0:T(8,128)(2,1)S(1)}, u32[]{:S(2)}, u32[]{:S(2)}) collective-permute-start(bf16[1728,128]{1,0:T(8,128)(2,1)S(1)} %bitcast.140), channel_id=1, source_target_pairs={{4,0},{8,4},{12,8},{16,12},{20,16},{24,20},{28,24},{5,1},{9,5},{13... | collective-permute-start | bytes 1327112 | tf_op jit(solution)/shard_map/ppermute | solution.py:28
  508.4 14.0 %collective-permute-start.5 = (bf16[1728,128]{1,0:T(8,128)(2,1)S(1)}, bf16[1728,128]{1,0:T(8,128)(2,1)S(1)}, u32[]{:S(2)}, u32[]{:S(2)}) collective-permute-start(bf16[1728,128]{1,0:T(8,128)(2,1)S(1)} %bitcast.143), channel_id=1, source_target_pairs={{1,0},{3,2},{5,4},{7,6},{9,8},{11,10},{13,12},{15,14},{17,16},{19,... | collective-permute-start | bytes 1327112 | tf_op jit(solution)/shard_map/ppermute | solution.py:28
  512.7 11.9 %collective-permute-start.3 = (bf16[1728,128]{1,0:T(8,128)(2,1)S(1)}, bf16[1728,128]{1,0:T(8,128)(2,1)S(1)}, u32[]{:S(2)}, u32[]{:S(2)}) collective-permute-start(bf16[1728,128]{1,0:T(8,128)(2,1)S(1)} %bitcast.144), channel_id=1, source_target_pairs={{0,4},{4,8},{8,12},{12,16},{16,20},{20,24},{24,28},{1,5},{5,9},{9,... | collective-permute-start | bytes 1327112 | tf_op jit(solution)/shard_map/ppermute | solution.py:23
  516.6 9.9 %collective-permute-start.4 = (bf16[1728,128]{1,0:T(8,128)(2,1)S(1)}, bf16[1728,128]{1,0:T(8,128)(2,1)S(1)}, u32[]{:S(2)}, u32[]{:S(2)}) collective-permute-start(bf16[1728,128]{1,0:T(8,128)(2,1)S(1)} %bitcast.145), channel_id=1, source_target_pairs={{4,0},{8,4},{12,8},{16,12},{20,16},{24,20},{28,24},{5,1},{9,5},{13... | collective-permute-start | bytes 1327112 | tf_op jit(solution)/shard_map/ppermute | solution.py:28
  520.8 13.8 %collective-permute-start.2 = (bf16[1728,128]{1,0:T(8,128)(2,1)S(1)}, bf16[1728,128]{1,0:T(8,128)(2,1)S(1)}, u32[]{:S(2)}, u32[]{:S(2)}) collective-permute-start(bf16[1728,128]{1,0:T(8,128)(2,1)S(1)} %bitcast.141), channel_id=1, source_target_pairs={{0,1},{2,3},{4,5},{6,7},{8,9},{10,11},{12,13},{14,15},{16,17},{18,... | collective-permute-start | bytes 1327112 | tf_op jit(solution)/shard_map/ppermute | solution.py:23
  (17 other events, 187.1 us)
Sparse Core Ops, SparseCore 0:
  75.3 44.2 reduce-scatter.22
  132.8 45.0 reduce-scatter.20
  180.2 42.3 reduce-scatter.18
  224.9 47.0 reduce-scatter.16
  274.2 42.3 reduce-scatter.14
  318.8 42.3 reduce-scatter.12
  363.5 42.3 reduce-scatter.10
  408.3 42.3 reduce-scatter.8
